TPU v7x, 32 devices: a whole 2x2x4 slice. The times are simulated.
32 devices in a mesh: gcm: 4 (over y, core), crm: 8 (over z, x).
Axes of the slice: x: 2, y: 2, z: 4, core: 2. Of those that a mesh axis runs over, the one named last changes fastest.
Arguments:
- tracer: float32 [72, 32, 2048], P(None, 'gcm', 'crm'), may hold values from -6 to 6
- wind_x: float32 [72, 32, 2048], P(None, 'gcm', 'crm'), may hold values from -4 to 4
- wind_y: float32 [72, 32, 2048], P(None, 'gcm', 'crm'), may hold values from -4 to 4
- drops: bfloat16 [4096, 33, 256], P(('gcm', 'crm')), may hold values from 0 to 1
- owner: int32 [4096, 1], P(('gcm', 'crm')), may hold values from 0 to 31, as said below
- counts: int32 [4096], P(('gcm', 'crm')), may hold values from 0 to 4, as said below
- collision: bfloat16 [33, 1089], replicated, may hold values from -0.1875 to 0.1875
- growth: float32 [33], replicated, may hold values from -4 to 4
Outputs:
- tracer_next: float32 [72, 32, 2048], P(None, 'gcm', 'crm')
- drops_next: bfloat16 [4096, 33, 256], P(('gcm', 'crm'))
- power: float32 [16, 8192], P(None, ('gcm', 'crm'))
Inputs may be any that keep to these rules, and one draw needn't show every extreme that they name: Owner index in gcm-then-crm device order; among the 128 columns of one device no owner appears more than 8 times, and some owner appears exactly 8 times. `counts`: how cloudy the columns are differs from device to device.
All inputs are finite; a program needn't handle non-finite values.
Results may differ from a plain program's by a relative error of at most 0.0018.
Values may be sent and summed in bfloat16 or wider, within the bound.
No kernel may reach another device: no remote copies, remote signals or barrier semaphores. Data moves between devices by JAX's collectives and lax.ppermute only.
A program may use at most 128 MiB of HBM per device.

v0:
```python
import functools

import jax
import jax.numpy as jnp
import numpy as np
from jax import lax
from jax.experimental import pallas as pl
from jax.experimental.pallas import tpu as pltpu
from jax.sharding import PartitionSpec as P

CRM_X = 16
CRM_LEV = 16
DYN_STEPS = 2

DT_DYN = 0.04
DT_CRM = 0.05
DT_PHYS = 0.5
HIGH = lax.Precision.HIGHEST
F32 = jnp.float32
BF16 = jnp.bfloat16
GROUP = 8
CHUNK = 8
MIB = 1024 * 1024


def gll_tables():
    inv_root = 1.0 / np.sqrt(5.0)
    gll_nodes = np.array([-1.0, -inv_root, inv_root, 1.0])
    weights = np.array([1.0, 5.0, 5.0, 1.0]) / 6.0
    legendre = (5.0 * gll_nodes**3 - 3.0 * gll_nodes) / 2.0
    derivative = np.zeros((4, 4))
    for i in range(4):
        for j in range(4):
            if i != j:
                derivative[i, j] = legendre[i] / (legendre[j] * (gll_nodes[i] - gll_nodes[j]))
    derivative[0, 0] = -3.0
    derivative[3, 3] = 3.0
    return (2.0 * derivative, weights)


def level_tables(levels, crm_levels):
    spacing = levels / crm_levels
    centres = (np.arange(crm_levels) + 0.5) * spacing - 0.5
    hats = np.maximum(0.0, 1.0 - np.abs(np.arange(levels)[None, :] - centres[:, None]) / spacing)
    down_map = hats / hats.sum(axis=1, keepdims=True)
    up_map = hats.T / hats.T.sum(axis=1, keepdims=True)
    return (down_map, up_map)


DERIV, WEIGHTS = gll_tables()


def iota(shape, axis):
    return lax.broadcasted_iota(jnp.int32, shape, axis)


def derivative_terms(shape, axis):
    phase = iota(shape, axis) % 4
    terms = []
    for shift in range(-3, 4):
        value = jnp.zeros(shape, F32)
        for i in range(4):
            if 0 <= i + shift < 4:
                value = jnp.where(phase == i, F32(DERIV[i, i + shift]), value)
        terms.append((shift, value))
    return terms


def along(x, terms, axis):
    size = x.shape[axis]
    total = None
    for shift, value in terms:
        moved = x if shift == 0 else pltpu.roll(x, (-shift) % size, axis)
        part = value[None] * moved
        total = part if total is None else total + part
    return total


def tendency(x, u, v, row_terms, col_terms):
    halves = []
    for h in range(x.shape[2] // 128):
        cut = slice(128 * h, 128 * h + 128)
        q = x[:, :, cut]
        grad_x = along(q, row_terms, 1)
        grad_y = along(q, col_terms, 2)
        halves.append(-(u[:, :, cut] * grad_x + v[:, :, cut] * grad_y))
    return jnp.concatenate(halves, axis=2)


def put_rows(x, levels, top_ref, bot_ref, i):
    top_ref[i, levels, :] = x[:, 0, :]
    bot_ref[i, levels, :] = x[:, 7, :]


def first_kernel(
    q_hbm, u_hbm, v_hbm, count_ref,
    tend_ref, top_ref, bot_ref, right_ref, left_ref, count_out_ref, q_ref, u_ref, v_ref, sems,
):
    row_terms = derivative_terms((8, 128), 0)
    col_terms = derivative_terms((8, 128), 1)
    lane = iota((8, 128), 1)
    count_out_ref[...] = count_ref[...]
    chunks = q_ref.shape[0] // CHUNK

    def copies(chunk):
        levels = pl.ds(pl.multiple_of(chunk * CHUNK, CHUNK), CHUNK)
        return [
            pltpu.make_async_copy(src.at[levels], dst.at[levels], sems.at[i, chunk])
            for i, (src, dst) in enumerate(((q_hbm, q_ref), (u_hbm, u_ref), (v_hbm, v_ref)))
        ]

    for chunk in range(chunks):
        for copy in copies(chunk):
            copy.start()

    def body(chunk, carry):
        for copy in copies(chunk):
            copy.wait()
        for half in range(CHUNK // 4):
            right = jnp.zeros((8, 128), F32)
            left = jnp.zeros((8, 128), F32)
            for j in range(4):
                for f, ref in enumerate((q_ref, u_ref, v_ref)):
                    start = 32 * j + 8 * f
                    here = (lane >= start) & (lane < start + 8)
                    x = ref[chunk * CHUNK + half * 4 + j]
                    moved = pltpu.roll(x[:, 128:256], (start - 120) % 128, 1)
                    right = jnp.where(here, moved, right)
                    first = x[:, 0:128]
                    if start:
                        first = pltpu.roll(first, start, 1)
                    left = jnp.where(here, first, left)
            right_ref[chunk * (CHUNK // 4) + half] = right
            left_ref[chunk * (CHUNK // 4) + half] = left
        levels = pl.ds(pl.multiple_of(chunk * CHUNK, CHUNK), CHUNK)
        q = q_ref[levels]
        tend = tendency(q, u_ref[levels], v_ref[levels], row_terms, col_terms)
        tend_ref[levels] = tend
        put_rows(tend, levels, top_ref, bot_ref, 0)
        put_rows(q, levels, top_ref, bot_ref, 1)
        return carry

    lax.fori_loop(0, chunks, body, 0)


def strip_kernel(
    left_ref, right_ref, top_main, bot_main,
    q_ref, u_ref, v_ref, tend_ref, top_ref, bot_ref,
):
    row_terms = derivative_terms((8, 128), 0)
    col_terms = derivative_terms((8, 128), 1)
    lane = iota((8, 128), 1)
    for out, main in ((top_ref, top_main), (bot_ref, bot_main)):
        out[:, 0:256] = main[0]
        out[:, 256:512] = main[1]

    def body(chunk, carry):
        tiles = [[], [], []]
        for half in range(CHUNK // 4):
            west = left_ref[chunk * (CHUNK // 4) + half]
            east = right_ref[chunk * (CHUNK // 4) + half]
            for j in range(4):
                for f in range(3):
                    start = 32 * j + 8 * f
                    a = pltpu.roll(east, 128 - start, 1) if start else east
                    b = pltpu.roll(west, (120 - start) % 128, 1)
                    tiles[f].append(jnp.where(lane < 8, a, jnp.where(lane >= 120, b, 0.0)))
        q, u, v = [jnp.stack(tile, axis=0) for tile in tiles]
        levels = pl.ds(pl.multiple_of(chunk * CHUNK, CHUNK), CHUNK)
        q_ref[levels] = q
        u_ref[levels] = u
        v_ref[levels] = v
        tend = tendency(q, u, v, row_terms, col_terms)
        tend_ref[levels] = tend
        shared = jnp.where((lane >= 8) & (lane < 24), pltpu.roll(q, 16, 2), tend)
        top_ref[levels, 512:640] = shared[:, 0, :]
        bot_ref[levels, 512:640] = shared[:, 7, :]
        return carry

    lax.fori_loop(0, q_ref.shape[0] // CHUNK, body, 0)


def assemble_chunk(x, up, down):
    shape = x.shape
    row = iota(shape, 1)
    partner = jnp.where(
        row == 0,
        jnp.broadcast_to(up[:, None, :], shape),
        jnp.where(
            row == 7,
            jnp.broadcast_to(down[:, None, :], shape),
            jnp.where(row == 3, pltpu.roll(x, 7, 1), pltpu.roll(x, 1, 1)),
        ),
    )
    x = jnp.where((row % 4 == 0) | (row % 4 == 3), 0.5 * (x + partner), x)
    col = iota(shape, 2)
    partner = jnp.where(
        col % 4 == 3, pltpu.roll(x, shape[2] - 1, 2), pltpu.roll(x, 1, 2)
    )
    return jnp.where((col % 4 == 0) | (col % 4 == 3), 0.5 * (x + partner), x)


def join(main, strip):
    return jnp.concatenate([main, strip], axis=2)


def second_kernel(
    q_ref, u_ref, v_ref, tend_ref, q_strip, u_strip, v_strip, tend_strip, up_ref, down_ref,
    state_ref, smooth_ref, next_ref, top_ref, bot_ref,
):
    row_terms = derivative_terms((8, 128), 0)
    col_terms = derivative_terms((8, 128), 1)

    def body(chunk, carry):
        levels = pl.ds(pl.multiple_of(chunk * CHUNK, CHUNK), CHUNK)
        q = join(q_ref[levels], q_strip[levels])
        rows = []
        for ref in (up_ref, down_ref):
            shared = ref[levels, 512:640]
            rows.append(jnp.concatenate([ref[levels, 0:256], shared], axis=1))
            rows.append(jnp.concatenate([ref[levels, 256:512], pltpu.roll(shared, 112, 1)], axis=1))
        change = assemble_chunk(join(tend_ref[levels], tend_strip[levels]), rows[0], rows[2])
        smooth = assemble_chunk(q, rows[1], rows[3])
        smooth_ref[levels] = smooth[:, :, 0:256]
        state = q + DT_DYN * change
        state_ref[levels] = state[:, :, 0:256]
        tend = tendency(
            state, join(u_ref[levels], u_strip[levels]), join(v_ref[levels], v_strip[levels]),
            row_terms, col_terms,
        )
        next_ref[levels] = tend
        put_rows(tend, levels, top_ref, bot_ref, 0)
        return carry

    lax.fori_loop(0, q_ref.shape[0] // CHUNK, body, 0)


def third_kernel(
    q_ref, state_ref, smooth_ref, tend_ref, up_ref, down_ref, down_map_ref, coef_ref, growth_ref,
    base_ref, forcing_ref, near_ref, far_ref,
):
    cols = forcing_ref.shape[1]
    half = cols // 2
    phase = iota((8, 256), 0) % 4
    row_weight = jnp.where((phase == 0) | (phase == 3), F32(WEIGHTS[0]), F32(WEIGHTS[1]))
    near_rows = jnp.where(iota((8, 256), 0) < 4, row_weight, 0.0)
    far_rows = row_weight - near_rows

    def body(chunk, carry):
        levels = pl.ds(pl.multiple_of(chunk * CHUNK, CHUNK), CHUNK)
        change = assemble_chunk(tend_ref[levels], up_ref[0, levels, :], down_ref[0, levels, :])
        moved = (state_ref[levels] + DT_DYN * change[:, :, 0:256]) - q_ref[levels]
        base_ref[levels] = smooth_ref[levels] + moved
        near_ref[levels, :] = jnp.sum(moved * near_rows[None], axis=1)
        far_ref[levels, :] = jnp.sum(moved * far_rows[None], axis=1)
        return carry

    lax.fori_loop(0, q_ref.shape[0] // CHUNK, body, 0)
    point = iota((256, cols), 0)
    element = iota((256, cols), 1)
    weight = jnp.where(
        (point % 4 == 0) | (point % 4 == 3), F32(WEIGHTS[0]), F32(WEIGHTS[1])
    ) * F32(0.25 / (DYN_STEPS * DT_DYN))
    near_cols = jnp.where(point // 4 == element, weight, 0.0)
    far_cols = jnp.where(point // 4 + half == element, weight, 0.0)
    means = jnp.dot(near_ref[...], near_cols, precision=HIGH, preferred_element_type=F32)
    means += jnp.dot(far_ref[...], far_cols, precision=HIGH, preferred_element_type=F32)
    forcing = jnp.dot(down_map_ref[...], means, precision=HIGH, preferred_element_type=F32)
    forcing_ref[...] = forcing.astype(BF16).astype(F32)


def coef_kernel(
    collision_ref, table_ref, growth_ref, after_ref, coef_ref, growth_out_ref, wide_ref, line_ref
):
    bins = collision_ref.shape[0]
    total = jnp.dot(collision_ref[...], table_ref[...], preferred_element_type=F32) * DT_CRM
    coarse = total.astype(BF16).astype(F32)
    wide_ref[...] = jnp.zeros(wide_ref.shape, F32)
    wide_ref[0:bins, :] = coarse
    wide_ref[40 : 40 + bins, :] = total - coarse
    coef_ref[...] = wide_ref[...].astype(BF16)
    line_ref[...] = jnp.zeros(line_ref.shape, F32)
    line_ref[0:1, 0:bins] = growth_ref[...]
    rows = jnp.broadcast_to(line_ref[0:1, :], (128, 128)).T[0:40]
    for h in range(growth_out_ref.shape[1] // 128):
        growth_out_ref[:, 128 * h : 128 * h + 128] = rows


def rank_row(values):
    total = values.shape[1]
    across = jnp.broadcast_to(values, (total, total))
    down = across.T
    earlier = iota((total, total), 0) < iota((total, total), 1)
    ahead = (down > across) | ((down == across) & earlier)
    return jnp.sum(ahead.astype(F32), axis=0, keepdims=True)


def plan_kernel(
    capacity, count_ref, other_ref, owner_ref, after_ref,
    sent_ref, order_ref, force_ref, ordered_ref, rank_ref, slot_ref,
):
    cols = count_ref.shape[1]
    counts = count_ref[...].astype(F32)
    others = other_ref[...].astype(F32)
    rank = rank_row(counts)
    other_rank = rank_row(others)
    square = (cols, cols)
    index = iota(square, 0).astype(F32)
    odd = 2.0 * iota(square, 1).astype(F32) + 1.0
    down_rank = jnp.broadcast_to(rank, square).T
    sent = jnp.sum(jnp.where(down_rank == odd, index, 0.0), axis=0, keepdims=True)
    sent_ref[...] = sent.astype(jnp.int32)
    rank_ref[...] = rank.astype(jnp.int32)

    is_odd = rank.astype(jnp.int32) % 2 == 1
    other_odd = other_rank.astype(jnp.int32) % 2 == 1
    listed = jnp.concatenate(
        [jnp.where(is_odd, -1.0, counts), jnp.where(other_odd, others, -1.0)], axis=1
    )
    lane = iota((1, cols), 1).astype(F32)
    name = jnp.concatenate([lane, cols + 0.5 * (other_rank - 1.0)], axis=1)
    wide = (2 * cols, 2 * cols)
    place = jnp.broadcast_to(rank_row(listed), wide).T[:, 0:cols]
    here = place == iota((2 * cols, cols), 1).astype(F32)
    force = iota((2 * cols, cols), 0).astype(F32)
    name = jnp.broadcast_to(name, wide).T[:, 0:cols]
    value = jnp.broadcast_to(listed, wide).T[:, 0:cols]
    for what, ref in ((name, order_ref), (force, force_ref), (value, ordered_ref)):
        total = jnp.sum(jnp.where(here, what, 0.0), axis=0, keepdims=True)
        ref[...] = total.astype(jnp.int32)

    owners = jnp.broadcast_to(owner_ref[...].astype(F32), square)
    same = (owners.T == owners) & (iota(square, 0) < iota(square, 1))
    earlier = jnp.sum(same.astype(F32), axis=0, keepdims=True)
    slot_ref[...] = owner_ref[...] * capacity + earlier.astype(jnp.int32)


def gather_kernel(sent_ref, drops_ref, out_ref, wide_ref):
    bins = drops_ref.shape[1]
    wide_ref[...] = jnp.zeros(wide_ref.shape, F32)

    def body(p, carry):
        for k in range(8):
            wide_ref[k, 0:bins, :] = drops_ref[sent_ref[0, 8 * p + k]].astype(F32)
        for k in range(8):
            out_ref[8 * p + k] = wide_ref[k].astype(BF16)
        return carry

    lax.fori_loop(0, out_ref.shape[0] // 8, body, 0)


def merge_kernel(sent_ref, final_ref, back_ref, out_ref):
    out_ref[...] = final_ref[...]

    def body(p, carry):
        row = back_ref[p].astype(F32)[0 : out_ref.shape[1]]
        out_ref[sent_ref[0, p]] = row.astype(BF16)
        return carry

    lax.fori_loop(0, back_ref.shape[0] - 1, body, 0)


def crm_kernel(
    order_ref, force_ref, count_ref, sent_ref,
    drops_ref, guest_ref, forcing_ref, other_ref, coef_ref, growth_ref,
    final_ref, back_ref, own_ref, away_ref,
    state_ref, start_ref, pair_ref, twice_ref, cell_ref, heat_cell_ref, echo_cell_ref,
):
    bins = drops_ref.shape[1]
    cells = drops_ref.shape[2]
    cols = drops_ref.shape[0]
    guests = guest_ref.shape[0]
    coef = coef_ref[...]
    growth = growth_ref[...]
    state_ref[...] = jnp.zeros(state_ref.shape, F32)
    heat_cell_ref[...] = jnp.zeros(heat_cell_ref.shape, F32)
    echo_cell_ref[...] = jnp.zeros(echo_cell_ref.shape, F32)
    mass = (iota((40, cells), 0) + 1).astype(F32) / F32(bins)
    spread = (iota((CRM_LEV, cells), 1) // CRM_X == iota((CRM_LEV, cells), 0)).astype(BF16)
    for i, ref in enumerate((forcing_ref, other_ref)):
        rows = jnp.dot(ref[...].T.astype(BF16), spread, preferred_element_type=F32)
        cell_ref[cols * i : cols * i + cols, :] = DT_CRM * rows

    def grow(k, which, zero):
        grown = state_ref[k] + growth * cell_ref[pl.ds(which, 1), :]
        for h in range(cells // 128):
            cut = slice(128 * h, 128 * h + 128)
            g = grown[0:32, cut]
            last = grown[32:40, cut]
            twice_ref[2 * k + h, 0:32, :] = g
            twice_ref[2 * k + h, 32:48, :] = g[0:16]
            for d in range(16):
                other = g if d % 8 == 0 else twice_ref[2 * k + h, pl.ds(zero + d, 32), :]
                if d == 8:
                    other = jnp.concatenate([g[8:], g[:8]], axis=0)
                pair_ref[k, 32 * d : 32 * d + 32, cut] = (g * other).astype(BF16)
            pair_ref[k, 512:528, cut] = (g[0:16] * g[16:32]).astype(BF16)
            pair_ref[k, 528:560, cut] = (g * last[0:1]).astype(BF16)
            tail = jnp.concatenate([last * last, jnp.zeros((8, 128), F32)], axis=0)
            pair_ref[k, 560:576, cut] = tail.astype(BF16)
        return grown

    def group(index, carry):
        base = index * GROUP
        which = [order_ref[0, base + k] for k in range(GROUP)]
        force = [force_ref[0, base + k] for k in range(GROUP)]
        count = [count_ref[0, base + k] for k in range(GROUP)]
        for k in range(GROUP):
            mine = drops_ref[jnp.minimum(which[k], cols - 1)].astype(F32)
            guest = guest_ref[jnp.clip(which[k] - cols, 0, guests - 1)].astype(F32)
            start = jnp.where(which[k] < cols, mine, guest[0:bins])
            start_ref[k, 0:bins, :] = start
            state_ref[k, 0:bins, :] = start

        zero = jnp.minimum(which[0], 0)

        def step(s, c):
            for k in range(GROUP):
                grown = grow(k, force[k], zero)
                change = jnp.dot(coef, pair_ref[k], preferred_element_type=F32)
                moved = grown + (change[0:40] + change[40:80])
                state_ref[k] = jnp.where(s < count[k], moved, state_ref[k])
            return c

        lax.fori_loop(0, count[0], step, 0)
        for k in range(GROUP):
            final = state_ref[k, 0:bins, :]
            weighted = mass[0:bins] * final
            heat = jnp.sum(mass[0:bins] * (final - start_ref[k, 0:bins, :]), axis=0, keepdims=True)
            echo = jnp.sum(weighted * weighted, axis=0, keepdims=True)
            heat_cell_ref[pl.ds(which[k], 1), :] = heat
            echo_cell_ref[pl.ds(which[k], 1), :] = echo

            result = state_ref[k].astype(BF16)
            guest = jnp.clip(which[k] - cols, 0, guests - 1)
            mine = which[k] < cols
            final_ref[jnp.where(mine, which[k], sent_ref[0, guest])] = final.astype(BF16)
            back_ref[jnp.where(mine, guests, guest)] = result
        return carry

    lax.fori_loop(0, cols // GROUP, group, 0)
    means = jnp.where(
        iota((CRM_LEV, cells), 1) // CRM_X == iota((CRM_LEV, cells), 0), F32(1.0 / CRM_X), 0.0
    )
    contract = (((1,), (1,)), ((), ()))
    heat = lax.dot_general(
        means, heat_cell_ref[...], contract, precision=HIGH, preferred_element_type=F32
    )
    heat = heat.astype(BF16).astype(F32)
    echo = lax.dot_general(
        means, echo_cell_ref[...], contract, precision=HIGH, preferred_element_type=F32
    )
    both = jnp.concatenate([heat, jnp.log(1.0 + echo)], axis=0)
    own_ref[...] = both[:, 0:cols]
    away_ref[...] = both[:, cols : 2 * cols]


def block_kernel(n_gcm, n_crm, own_ref, back_ref, rank_ref, slot_ref, heat_ref, send_ref):
    cols = own_ref.shape[1]
    odd = 2 * iota((cols, cols), 0) + 1
    home = (rank_ref[...] == odd).astype(F32)
    both = own_ref[...] + jnp.dot(
        back_ref[...], home, precision=HIGH, preferred_element_type=F32
    )
    heat = both[0:CRM_LEV]
    echo = both[CRM_LEV:]
    heat_ref[...] = heat
    contract = (((1,), (1,)), ((), ()))
    devices = send_ref.shape[0]
    slots = 2 * cols
    capacity = slots // devices
    onehot = (slot_ref[...] == iota((slots, cols), 0)).astype(F32)
    packed = lax.dot_general(echo, onehot, contract, precision=HIGH, preferred_element_type=F32)
    coarse = packed.astype(BF16).astype(F32)
    rest = packed - coarse
    middle = rest.astype(BF16).astype(F32)
    pieces = (coarse, middle, rest - middle)
    lane = iota((CRM_LEV, 128), 1)
    near = heat
    far = pltpu.roll(heat, 64, 1)
    sides = jnp.where(
        lane == 1, pltpu.roll(heat, 65, 1), jnp.where(lane == 62, pltpu.roll(heat, 63, 1), heat)
    )
    g = lax.axis_index("gcm")
    for d in range(devices):
        away = d // n_crm - g
        below = (away == 1) | (away == 1 - n_gcm)
        above = (away == -1) | (away == n_gcm - 1)
        block = jnp.where(below, far, jnp.where(above, near, sides))
        tile, offset = divmod(d * capacity, 128)
        for i, piece in enumerate(pieces):
            moved = pltpu.roll(
                piece[:, 128 * tile : 128 * tile + 128], (64 + i * capacity - offset) % 128, 1
            )
            start = 64 + i * capacity
            block = jnp.where((lane >= start) & (lane < start + capacity), moved, block)
        send_ref[d] = block.astype(BF16)


def last_kernel(
    n_gcm, n_crm, base_ref, own_ref, got_ref, up_map_ref, drops_in, out_ref, power_ref, drops_out,
    *back_refs,
):
    cols = own_ref.shape[1]
    half = cols // 2
    element = iota((cols, 256), 0)
    col = iota((cols, 256), 1)
    phase = col % 4
    edge = (phase == 0) | (phase == 3)
    other = jnp.where(phase == 0, col // 4 - 1, col // 4 + 1)

    def spread(centre, start, west, west_lane, east, east_lane):
        inside = jnp.where(element == col // 4 + start, jnp.where(edge, 0.5, 1.0), 0.0)
        beside = edge & (element == other + start) & (other >= 0) & (other < half)
        middle = jnp.where(beside, 0.5, inside).astype(BF16)
        from_west = jnp.where((col == 0) & (element == west_lane), 0.5, 0.0).astype(BF16)
        from_east = jnp.where((col == 255) & (element == east_lane), 0.5, 0.0).astype(BF16)
        total = jnp.dot(centre, middle, preferred_element_type=F32)
        total += jnp.dot(west, from_west, preferred_element_type=F32)
        total += jnp.dot(east, from_east, preferred_element_type=F32)
        return total

    own = own_ref[...].astype(BF16)
    g = lax.axis_index("gcm")
    c = lax.axis_index("crm")
    north = jnp.where(g == 0, n_gcm - 1, g - 1) * n_crm
    south = jnp.where(g == n_gcm - 1, 0, g + 1) * n_crm
    west = jnp.where(c == 0, n_crm - 1, c - 1)
    east = jnp.where(c == n_crm - 1, 0, c + 1)
    up, down = got_ref[north + c], got_ref[south + c]
    left, right = got_ref[g * n_crm + west], got_ref[g * n_crm + east]
    up_left, up_right = got_ref[north + west], got_ref[north + east]
    down_left, down_right = got_ref[south + west], got_ref[south + east]
    above = spread(up, 0, up_left, half - 1, up_right, 0)
    near = spread(own, 0, left, half - 1, right, 0)
    far = spread(own, half, left, half - 2, right, 1)
    below = spread(down, 0, down_left, half - 1, down_right, 0)
    parts = (
        0.5 * (above + near), near, 0.5 * (near + far), far, 0.5 * (far + below),
    )
    up_map = up_map_ref[...]
    for part, ref in zip(parts, back_refs):
        ref[...] = DT_PHYS * jnp.dot(up_map, part, precision=HIGH, preferred_element_type=F32)

    devices = got_ref.shape[0]
    slots = power_ref.shape[1]
    capacity = slots // devices
    lane = iota((CRM_LEV, 128), 1)
    tiles = [jnp.zeros((CRM_LEV, 128), F32) for _ in range(slots // 128)]
    for d in range(devices):
        block = got_ref[d].astype(F32)
        fine = pltpu.roll(block, 128 - 2 * capacity, 1) + pltpu.roll(block, 128 - capacity, 1)
        tile, offset = divmod(d * capacity, 128)
        moved = pltpu.roll(block + fine, (offset - 64) % 128, 1)
        tiles[tile] = jnp.where((lane >= offset) & (lane < offset + capacity), moved, tiles[tile])
    power_ref[...] = jnp.concatenate(tiles, axis=1)

    def body(chunk, carry):
        levels = pl.ds(pl.multiple_of(chunk * CHUNK, CHUNK), CHUNK)
        shape = (CHUNK, 8, 256)
        row = iota(shape, 1)
        wide = [jnp.broadcast_to(ref[levels, :][:, None, :], shape) for ref in back_refs]
        back = jnp.where(
            row == 0,
            wide[0],
            jnp.where(
                row < 3,
                wide[1],
                jnp.where(row < 5, wide[2], jnp.where(row < 7, wide[3], wide[4])),
            ),
        )
        out_ref[levels] = base_ref[levels] + back
        return carry

    lax.fori_loop(0, base_ref.shape[0] // CHUNK, body, 0)


def call(kernel, outs, args, scratch=(), sems=(), flops=10_000_000, limit=16, through=()):
    spaces = {
        "s": pl.BlockSpec(memory_space=pltpu.SMEM),
        "v": pl.BlockSpec(memory_space=pltpu.VMEM),
        "h": pl.BlockSpec(memory_space=pl.ANY),
    }
    return pl.pallas_call(
        kernel,
        out_shape=[jax.ShapeDtypeStruct(s, t) for s, t in outs]
        + [jax.ShapeDtypeStruct(args[i][1].shape, args[i][1].dtype) for i in through],
        in_specs=[spaces[kind] for kind, _ in args],
        out_specs=[spaces["v"]] * len(outs) + [spaces["h"]] * len(through),
        input_output_aliases={i: len(outs) + n for n, i in enumerate(through)},
        scratch_shapes=[pltpu.VMEM(s, t) for s, t in scratch] + list(sems),
        compiler_params=pltpu.CompilerParams(vmem_limit_bytes=limit * MIB),
        cost_estimate=pl.CostEstimate(flops=flops, bytes_accessed=4_000_000, transcendentals=0),
    )(*[value for _, value in args])


def v(*values):
    return [("v", value) for value in values]


def shift(value, rows, cols):
    n_gcm = lax.axis_size("gcm")
    n_crm = lax.axis_size("crm")
    pairs = []
    for g in range(n_gcm):
        for c in range(n_crm):
            target = ((g + rows) % n_gcm) * n_crm + (c + cols) % n_crm
            pairs.append((g * n_crm + c, target))
    return lax.ppermute(value, ("gcm", "crm"), pairs)


def pair_table(bins):
    table = np.zeros((bins * bins, 576), np.float32)

    def put(column, i, j):
        table[i * bins + j, column] = 1.0
        table[j * bins + i, column] = 1.0

    for d in range(16):
        for b in range(32):
            put(32 * d + b, b, (b + d) % 32)
    for b in range(16):
        put(512 + b, b, b + 16)
    for b in range(32):
        put(528 + b, b, 32)
    put(560, 32, 32)
    return table


def to_partner(value):
    n_gcm = lax.axis_size("gcm")
    n_crm = lax.axis_size("crm")
    pairs = []
    for g in range(n_gcm):
        for c in range(n_crm):
            pairs.append((g * n_crm + c, (g ^ 1) * n_crm + c))
    return lax.ppermute(value, ("gcm", "crm"), pairs)


def shards(tracer, wind_x, wind_y, drops, owner, counts, collision, growth):
    devices = lax.axis_size("gcm") * lax.axis_size("crm")
    levels, row_count, col_count = tracer.shape
    col_total, bins, cells = drops.shape
    field = (tracer.shape, F32)
    strip = ((levels, row_count, 128), F32)
    rows = ((2, levels, col_count), F32)
    wide = col_count + 128
    down_map, up_map = level_tables(levels, CRM_LEV)

    row = ((1, col_total), jnp.int32)
    capacity = 2 * col_total // devices
    guests = col_total // 2
    tend, top, bot, to_right, to_left, count_row = call(
        first_kernel,
        [field, rows, rows] + [((levels // 4, 8, 128), F32)] * 2 + [row],
        [("h", tracer), ("h", wind_x), ("h", wind_y)] + v(counts[None, :]),
        [field] * 3,
        [pltpu.SemaphoreType.DMA((3, levels // CHUNK))],
        limit=62,
    )
    from_left = shift(to_right, 0, 1)
    from_right = shift(to_left, 0, -1)
    other_counts = to_partner(count_row)
    q_strip, u_strip, v_strip, tend_strip, top, bot = call(
        strip_kernel,
        [strip] * 4 + [((levels, wide + col_count), F32)] * 2,
        v(from_left, from_right, top, bot),
    )
    sent, order, force, ordered, rank, slot = call(
        functools.partial(plan_kernel, capacity),
        [row] * 6,
        v(count_row, other_counts, owner.T) + [("h", top)],
    )
    (leaving,) = call(
        gather_kernel,
        [((guests, 40, cells), BF16)],
        [("s", sent)] + v(drops),
        [((8, 40, cells), F32)],
    )
    guest_drops = to_partner(leaving)
    coef, growth_rows = call(
        coef_kernel,
        [((80, 576), BF16), ((40, cells), F32)],
        v(collision, jnp.asarray(pair_table(bins), BF16), growth[None, :]) + [("h", top)],
        [((80, 576), F32), ((8, 128), F32)],
    )
    state, smooth, tend, top, bot = call(
        second_kernel,
        [field, field, ((levels, row_count, wide), F32)] + [((1, levels, wide), F32)] * 2,
        v(tracer, wind_x, wind_y, tend, q_strip, u_strip, v_strip, tend_strip)
        + v(shift(bot, 1, 0), shift(top, -1, 0)),
    )
    base, forcing = call(
        third_kernel,
        [field, ((CRM_LEV, col_total), F32)],
        v(tracer, state, smooth, tend, shift(bot, 1, 0), shift(top, -1, 0))
        + v(jnp.asarray(down_map, F32)) + [("h", coef), ("h", growth_rows)],
        [((levels, col_count), F32), ((levels, col_count), F32)],
    )

    other_forcing = to_partner(forcing)
    n_gcm = lax.axis_size("gcm")
    n_crm = lax.axis_size("crm")

    pairs = ((2 * CRM_LEV, col_total), F32)
    final, back, own, away = call(
        crm_kernel,
        [((col_total, bins, cells), BF16), ((guests + 1, 40, cells), BF16), pairs, pairs],
        [("s", order), ("s", force), ("s", ordered), ("s", sent)]
        + v(drops, guest_drops, forcing, other_forcing, coef, growth_rows),
        [((GROUP, 40, cells), F32), ((GROUP, 40, cells), F32), ((GROUP, 576, cells), BF16),
         ((2 * GROUP, 48, 128), F32), ((2 * col_total, cells), F32),
         ((2 * col_total, cells), F32), ((2 * col_total, cells), F32)],
        flops=10_000_000_000,
        limit=24,
    )
    returned = to_partner(away)
    returned_drops = to_partner(back)
    heat, send = call(
        functools.partial(block_kernel, n_gcm, n_crm),
        [((CRM_LEV, col_total), F32), ((devices, CRM_LEV, 128), BF16)],
        v(own, returned, rank, slot),
    )
    got = lax.all_to_all(send, ("gcm", "crm"), split_axis=0, concat_axis=0, tiled=True)
    (drops_next,) = call(
        merge_kernel,
        [((col_total, bins, cells), BF16)],
        [("s", sent)] + v(final, returned_drops),
    )
    tracer_next, power, by_bin = call(
        functools.partial(last_kernel, n_gcm, n_crm),
        [field, ((CRM_LEV, devices * capacity), F32)],
        v(base, heat, got, jnp.asarray(up_map, F32))
        + [("h", drops_next.transpose(1, 0, 2))],
        [((levels, col_count), F32)] * 5,
        through=(4,),
    )
    drops_next = by_bin.transpose(1, 0, 2)
    return (tracer_next, drops_next, power)


def solution(mesh):
    return jax.shard_map(
        shards,
        mesh=mesh,
        in_specs=(
            P(None, "gcm", "crm"),
            P(None, "gcm", "crm"),
            P(None, "gcm", "crm"),
            P(("gcm", "crm"), None, None),
            P(("gcm", "crm"), None),
            P(("gcm", "crm")),
            P(),
            P(),
        ),
        out_specs=(P(None, "gcm", "crm"), P(("gcm", "crm"), None, None), P(None, ("gcm", "crm"))),
        check_vma=False,
    )
```

profile of v0, /device:TPU:0, one launch (start us, length us, event | category | flops | bytes accessed | tf_op | source)
XLA Modules:
  0.0 87.1 jit_solution(14629635822077617565)
XLA Ops:
  0.6 4.8 %shard_map.130 = (f32[72,8,256]{2,1,0:T(8,128)}, f32[2,72,256]{2,1,0:T(8,128)}, f32[2,72,256]{2,1,0:T(8,128)}, f32[18,8,128]{2,1,0:T(8,128)}, f32[18,8,128]{2,1,0:T(8,128)}, /*index=5*/s32[1,128]{1,0:T(1,128)}) custom-call(f32[72,8,256]{2,1,0:T(8,128)} %q_ref.3, f32[72,8,256]{2,1,0:T(8,128)} %u_ref.1, f32[72,8,256]{2,1,0:T(8,128)} %v_ref.1, s32[1,128]{1,0:T(1,128)} %bitcast.11), custom_call_target="tpu_custom_call" | custom-call | flops 10000000 | bytes 4000000 | tf_op jit(solution)/shard_map/pallas_call | solution.py:584
  5.4 3.0 %collective-permute-start = (f32[18,8,128]{2,1,0:T(8,128)}, f32[18,8,128]{2,1,0:T(8,128)S(1)}, u32[]{:S(2)}, u32[]{:S(2)}) collective-permute-start(f32[18,8,128]{2,1,0:T(8,128)} %get-tuple-element.40), channel_id=1, source_target_pairs={{0,1},{1,2},{2,3},{3,4},{4,5},{5,6},{6,7},{7,0},{8,9},{9,10},{10,1... | collective-permute-start | bytes 221192 | tf_op jit(solution)/shard_map/ppermute | solution.py:609
  8.4 3.1 %collective-permute-start.1 = (f32[18,8,128]{2,1,0:T(8,128)}, f32[18,8,128]{2,1,0:T(8,128)S(1)}, u32[]{:S(2)}, u32[]{:S(2)}) collective-permute-start(f32[18,8,128]{2,1,0:T(8,128)} %get-tuple-element.41), channel_id=1, source_target_pairs={{0,7},{1,0},{2,1},{3,2},{4,3},{5,4},{6,5},{7,6},{8,15},{9,8},{10,9... | collective-permute-start | bytes 221192 | tf_op jit(solution)/shard_map/ppermute | solution.py:609
  11.5 0.1 collective-permute-start.6
  11.6 2.9 %copy.16.drops_ref = bf16[128,33,256]{2,1,0:T(8,128)(2,1)S(1)} copy(bf16[128,33,256]{2,0,1:T(8,128)(2,1)} %param.14) | data formatting | bytes 4325376 | tf_op args[3]
  14.6 0.0 collective-permute-done.left_ref
  14.6 0.0 collective-permute-done.1.right_ref
  14.6 2.0 %shard_map.131 = (f32[72,8,128]{2,1,0:T(8,128)S(1)}, f32[72,8,128]{2,1,0:T(8,128)S(1)}, f32[72,8,128]{2,1,0:T(8,128)S(1)}, f32[72,8,128]{2,1,0:T(8,128)S(1)}, f3...) custom-call(f32[18,8,128]{2,1,0:T(8,128)S(1)} %collective-permute-done.left_ref, ...), custom_call_target="tpu_custom_call" | custom-call | flops 10000000 | bytes 4000000 | tf_op jit(solution)/shard_map/pallas_call | solution.py:584
  16.6 0.0 copy-start
  16.6 0.0 copy-start.1
  16.6 0.0 copy-start.2
  16.6 0.0 copy-start.4
  16.7 0.0 collective-permute-done.6.other_ref
  16.7 0.4 shard_map.135
  17.1 0.7 shard_map.136
  17.8 0.0 copy-start.3
  17.8 0.0 copy-start.7
  17.9 0.0 copy-start.11
  17.9 0.5 collective-permute-start.7
  18.4 0.1 collective-permute-start.2
  18.4 1.6 %collective-permute-start.3 = (f32[72,640]{1,0:T(8,128)S(1)}, f32[72,640]{1,0:T(8,128)S(1)}, u32[]{:S(2)}, u32[]{:S(2)}) collective-permute-start(f32[72,640]{1,0:T(8,128)S(1)} %get-tuple-element.49.after_ref), channel_id=1, source_target_pairs={{0,24},{1,25},{2,26},{3,27},{4,28},{5,29},{6,30},{7,31},{8,0},{9,1... | collective-permute-start | bytes 552968 | tf_op jit(solution)/shard_map/ppermute | solution.py:609
  20.1 3.2 %collective-permute-done.2.up_ref = f32[72,640]{1,0:T(8,128)S(1)} collective-permute-done((f32[72,640]{1,0:T(8,128)S(1)}, f32[72,640]{1,0:T(8,128)S(1)}, u32[]{:S(2)}, u32[]{:S(2)}) %collective-permute-start.2) | collective-permute-done | bytes 184352 | tf_op jit(solution)/shard_map/ppermute | solution.py:609
  23.3 1.1 %collective-permute-done.3.down_ref = f32[72,640]{1,0:T(8,128)S(1)} collective-permute-done((f32[72,640]{1,0:T(8,128)S(1)}, f32[72,640]{1,0:T(8,128)S(1)}, u32[]{:S(2)}, u32[]{:S(2)}) %collective-permute-start.3) | collective-permute-done | bytes 184352 | tf_op jit(solution)/shard_map/ppermute | solution.py:609
  24.5 0.0 copy-start.9
  24.5 3.3 %shard_map.132 = (f32[72,8,256]{2,1,0:T(8,128)S(1)}, f32[72,8,256]{2,1,0:T(8,128)S(1)}, f32[72,8,384]{2,1,0:T(8,128)S(1)}, f32[1,72,384]{2,1,0:T(8,128)S(1)}, f32[1,72,384]{2,1,0:T(8,128)S(1)}) custom-call(f32[72,8,256]{2,1,0:T(8,128)S(1)} %copy-done, f32[72,8,256]{2,1,0:T(8,128)S(1)} %copy-done.1, f32[72,8,256]{2,1,0:T(8,128)S(1)} %copy-done.2, ...), custom_call_target="tpu_custom_call" | custom-call | flops 10000000 | bytes 4000000 | tf_op jit(solution)/shard_map/pallas_call | solution.py:584
  27.8 0.7 collective-permute-start.4
  28.5 1.3 %collective-permute-start.5 = (f32[1,72,384]{2,1,0:T(8,128)S(1)}, f32[1,72,384]{2,1,0:T(8,128)S(1)}, u32[]{:S(2)}, u32[]{:S(2)}) collective-permute-start(f32[1,72,384]{2,1,0:T(8,128)S(1)} %get-tuple-element.54), channel_id=1, source_target_pairs={{0,24},{1,25},{2,26},{3,27},{4,28},{5,29},{6,30},{7,31},{8,0},{9,1... | collective-permute-start | bytes 331784 | tf_op jit(solution)/shard_map/ppermute | solution.py:609
  29.8 0.0 copy-done.3
  29.8 0.0 copy-done.11
  29.8 0.4 shard_map.133
  30.2 2.0 %collective-permute-done.4.up_ref = f32[1,72,384]{2,1,0:T(8,128)S(1)} collective-permute-done((f32[1,72,384]{2,1,0:T(8,128)S(1)}, f32[1,72,384]{2,1,0:T(8,128)S(1)}, u32[]{:S(2)}, u32[]{:S(2)}) %collective-permute-start.4) | collective-permute-done | bytes 110624 | tf_op jit(solution)/shard_map/ppermute | solution.py:609
  32.2 0.4 collective-permute-done.5.down_ref
  32.6 1.8 %shard_map.134 = (f32[72,8,256]{2,1,0:T(8,128)S(1)}, f32[16,128]{1,0:T(8,128)S(1)}) custom-call(f32[72,8,256]{2,1,0:T(8,128)S(1)} %copy-done, f32[72,8,256]{2,1,0:T(8,128)S(1)} %get-tuple-element.50.state_ref, f32[72,8,256]{2,1,0:T(8,128)S(1)} %get-tuple-element.51.smooth_ref, f32[72,8,384]{2,1,0:T(8,128)S(1)} %get-tuple-element.52.tend_ref, ...), custom_call_target="tpu_custom_call" | custom-call | flops 10000000 | bytes 4000000 | tf_op jit(solution)/shard_map/pallas_call | solution.py:584
  34.4 1.5 %collective-permute-start.8 = (f32[16,128]{1,0:T(8,128)S(1)}, f32[16,128]{1,0:T(8,128)S(1)}, u32[]{:S(2)}, u32[]{:S(2)}) collective-permute-start(f32[16,128]{1,0:T(8,128)S(1)} %get-tuple-element.63.forcing_ref), channel_id=1, source_target_pairs={{0,8},{1,9},{2,10},{3,11},{4,12},{5,13},{6,14},{7,15},{8,0},{9,1},... | collective-permute-start | bytes 24584 | tf_op jit(solution)/shard_map/ppermute | solution.py:637
  35.8 0.8 collective-permute-done.8.other_ref
  36.7 0.0 collective-permute-done.7.guest_ref
  36.7 30.6 %shard_map.137 = (bf16[128,33,256]{2,1,0:T(8,128)(2,1)S(1)}, bf16[65,40,256]{2,1,0:T(8,128)(2,1)}, f32[32,128]{1,0:T(8,128)S(1)}, f32[32,128]{1,0:T(8,128)S(1)}) custom-call(s32[1,128]{1,0:T(1,128)S(1)} %get-tuple-element.59.order_ref, s32[1,128]{1,0:T(1,128)S(1)} %get-tuple-element.60.force_ref, s32[1,128]{1,0:T(1,128)S(1)} %get-tuple-element.61.count_ref, ...), custom_call_target="tpu_custom_call" | custom-call | flops 10000000000 | bytes 4000000 | tf_op jit(solution)/shard_map/pallas_call | solution.py:584
  67.3 0.4 collective-permute-start.10
  67.6 0.1 collective-permute-start.9
  67.8 2.6 %collective-permute-done.9.back_ref = f32[32,128]{1,0:T(8,128)S(1)} collective-permute-done((f32[32,128]{1,0:T(8,128)S(1)}, f32[32,128]{1,0:T(8,128)S(1)}, u32[]{:S(2)}, u32[]{:S(2)}) %collective-permute-start.9) | collective-permute-done | bytes 16416 | tf_op jit(solution)/shard_map/ppermute | solution.py:637
  70.4 1.3 %shard_map.138 = (f32[16,128]{1,0:T(8,128)S(1)}, bf16[32,16,128]{2,1,0:T(8,128)(2,1)}) custom-call(f32[32,128]{1,0:T(8,128)S(1)} %get-tuple-element.64.own_ref, f32[32,128]{1,0:T(8,128)S(1)} %collective-permute-done.9.back_ref, s32[1,128]{1,0:T(1,128)S(1)} %get-tuple-element.66.rank_ref, s32[1,128]{1,0:T(1,128)S(1)} %get-tuple-element.67.slot_ref), custom_call_target="tpu_custom_call" | custom-call | flops 10000000 | bytes 4000000 | tf_op jit(solution)/shard_map/pallas_call | solution.py:584
  71.7 5.9 %all-to-all-start = ((bf16[32,16,128]{2,1,0:T(8,128)(2,1)}), bf16[32,16,128]{2,1,0:T(8,128)(2,1)S(1)}, u32[]{:S(2)}, u32[]{:S(2)}) async-start(bf16[32,16,128]{2,1,0:T(8,128)(2,1)} %get-tuple-element.69), calls=%async_computation | async-start | bytes 262144 | tf_op jit(solution)/shard_map/all_to_all | solution.py:724
  77.6 0.0 collective-permute-done.10.back_ref
  77.6 2.0 %shard_map.139 = bf16[128,33,256]{2,1,0:T(8,128)(2,1)S(1)} custom-call(s32[1,128]{1,0:T(1,128)S(1)} %get-tuple-element.62.sent_ref, bf16[128,33,256]{2,1,0:T(8,128)(2,1)S(1)} %get-tuple-element.70.final_ref, bf16[65,40,256]{2,1,0:T(8,128)(2,1)} %collective-permute-done.10.back_ref), custom_call_target="tpu_custom_call" | custom-call | flops 10000000 | bytes 4000000 | tf_op jit(solution)/shard_map/pallas_call | solution.py:584
  79.5 0.0 copy-start.8
  79.6 1.8 %copy.19 = bf16[128,33,256]{2,0,1:T(8,128)(2,1)} copy(bf16[128,33,256]{2,1,0:T(8,128)(2,1)S(1)} %shard_map.139) | data formatting | bytes 4325376 | tf_op jit(solution)/shard_map/pallas_call | solution.py:584
  81.4 3.9 %all-to-all-done.got_ref = bf16[32,16,128]{2,1,0:T(8,128)(2,1)S(1)} async-done(((bf16[32,16,128]{2,1,0:T(8,128)(2,1)}), bf16[32,16,128]{2,1,0:T(8,128)(2,1)S(1)}, u32[]{:S(2)}, u32[]{:S(2)}) %all-to-all-start) | async-done | bytes 131104 | tf_op jit(solution)/shard_map/all_to_all | solution.py:724
  85.3 1.8 %shard_map.140 = (f32[72,8,256]{2,1,0:T(8,128)}, f32[16,256]{1,0:T(8,128)}, bf16[33,128,256]{2,1,0:T(8,128)(2,1)}) custom-call(f32[72,8,256]{2,1,0:T(8,128)S(1)} %get-tuple-element.57.base_ref, f32[16,128]{1,0:T(8,128)S(1)} %get-tuple-element.68.own_ref, bf16[32,16,128]{2,1,0:T(8,128)(2,1)S(1)} %all-to-all-done.got_ref, ...), custom_call_target="tpu_custom_call", output_to_operand_aliasing={{2}: (4, {})} | custom-call | flops 10000000 | bytes 4000000 | tf_op jit(solution)/shard_map/pallas_call | solution.py:584
  (15 shorter events, 0.0 us)
Async XLA Ops:
  5.4 9.1 %collective-permute-start = (f32[18,8,128]{2,1,0:T(8,128)}, f32[18,8,128]{2,1,0:T(8,128)S(1)}, u32[]{:S(2)}, u32[]{:S(2)}) collective-permute-start(f32[18,8,128]{2,1,0:T(8,128)} %get-tuple-element.40), channel_id=1, source_target_pairs={{0,1},{1,2},{2,3},{3,4},{4,5},{5,6},{6,7},{7,0},{8,9},{9,10},{10,1... | collective-permute-start | bytes 221192 | tf_op jit(solution)/shard_map/ppermute | solution.py:609
  8.4 6.2 %collective-permute-start.1 = (f32[18,8,128]{2,1,0:T(8,128)}, f32[18,8,128]{2,1,0:T(8,128)S(1)}, u32[]{:S(2)}, u32[]{:S(2)}) collective-permute-start(f32[18,8,128]{2,1,0:T(8,128)} %get-tuple-element.41), channel_id=1, source_target_pairs={{0,7},{1,0},{2,1},{3,2},{4,3},{5,4},{6,5},{7,6},{8,15},{9,8},{10,9... | collective-permute-start | bytes 221192 | tf_op jit(solution)/shard_map/ppermute | solution.py:609
  11.5 3.1 %copy-start.5 = (f32[2,72,256]{2,1,0:T(8,128)S(1)}, f32[2,72,256]{2,1,0:T(8,128)}, u32[]{:S(2)}) copy-start(f32[2,72,256]{2,1,0:T(8,128)} %get-tuple-element.42.top_main) | copy-start | bytes 442372
  11.5 3.1 %copy-start.6 = (f32[2,72,256]{2,1,0:T(8,128)S(1)}, f32[2,72,256]{2,1,0:T(8,128)}, u32[]{:S(2)}) copy-start(f32[2,72,256]{2,1,0:T(8,128)} %get-tuple-element.43.bot_main) | copy-start | bytes 442372
  11.5 5.1 %copy-start.10 = (s32[128,1]{0,1:T(1,128)S(1)}, s32[128,1]{0,1:T(1,128)}, u32[]{:S(2)}) copy-start(s32[128,1]{0,1:T(1,128)} %param.15) | copy-start | bytes 1540
  11.5 5.2 %copy-start.12 = (s32[1,128]{1,0:T(1,128)S(1)}, s32[1,128]{1,0:T(1,128)}, u32[]{:S(2)}) copy-start(s32[1,128]{1,0:T(1,128)} %get-tuple-element.58.count_ref) | copy-start | bytes 1540
  11.5 5.1 %collective-permute-start.6 = (s32[1,128]{1,0:T(1,128)}, s32[1,128]{1,0:T(1,128)S(1)}, u32[]{:S(2)}, u32[]{:S(2)}) collective-permute-start(s32[1,128]{1,0:T(1,128)} %get-tuple-element.58.count_ref), channel_id=1, source_target_pairs={{0,8},{1,9},{2,10},{3,11},{4,12},{5,13},{6,14},{7,15},{8,0},{9,1},... | collective-permute-start | bytes 1544 | tf_op jit(solution)/shard_map/ppermute | solution.py:637
  16.6 7.8 %copy-start = (f32[72,8,256]{2,1,0:T(8,128)S(1)}, f32[72,8,256]{2,1,0:T(8,128)}, u32[]{:S(2)}) copy-start(f32[72,8,256]{2,1,0:T(8,128)} %q_ref.3) | copy-start | bytes 1769476
  16.6 7.8 %copy-start.1 = (f32[72,8,256]{2,1,0:T(8,128)S(1)}, f32[72,8,256]{2,1,0:T(8,128)}, u32[]{:S(2)}) copy-start(f32[72,8,256]{2,1,0:T(8,128)} %u_ref.1) | copy-start | bytes 1769476
  16.6 7.8 %copy-start.2 = (f32[72,8,256]{2,1,0:T(8,128)S(1)}, f32[72,8,256]{2,1,0:T(8,128)}, u32[]{:S(2)}) copy-start(f32[72,8,256]{2,1,0:T(8,128)} %v_ref.1) | copy-start | bytes 1769476
  16.6 7.8 %copy-start.4 = (f32[72,8,256]{2,1,0:T(8,128)S(1)}, f32[72,8,256]{2,1,0:T(8,128)}, u32[]{:S(2)}) copy-start(f32[72,8,256]{2,1,0:T(8,128)} %get-tuple-element.39.tend_ref) | copy-start | bytes 1769476
  17.8 12.0 %copy-start.3 = (bf16[1089,576]{1,0:T(8,128)(2,1)S(1)}, bf16[1089,576]{1,0:T(8,128)(2,1)}, u32[]{:S(2)}) copy-start(bf16[1089,576]{1,0:T(8,128)(2,1)} %constant.6.clone.table_ref) | copy-start | bytes 3763588
  17.8 12.0 %copy-start.7 = (bf16[33,1089]{1,0:T(8,128)(2,1)S(1)}, bf16[33,1089]{1,0:T(8,128)(2,1)}, u32[]{:S(2)}) copy-start(bf16[33,1089]{1,0:T(8,128)(2,1)} %collision_ref.1) | copy-start | bytes 215626
  17.9 12.0 %copy-start.11 = (f32[33]{0:T(128)S(1)}, f32[33]{0:T(128)}, u32[]{:S(2)}) copy-start(f32[33]{0:T(128)} %param.18) | copy-start | bytes 400
  17.9 18.8 %collective-permute-start.7 = (bf16[64,40,256]{2,1,0:T(8,128)(2,1)S(1)}, bf16[64,40,256]{2,1,0:T(8,128)(2,1)S(1)}, u32[]{:S(2)}, u32[]{:S(2)}) collective-permute-start(bf16[64,40,256]{2,1,0:T(8,128)(2,1)S(1)} %shard_map.136), channel_id=1, source_target_pairs={{0,8},{1,9},{2,10},{3,11},{4,12},{5,13},{6,14},{7,15},{8,0},{9,1},... | collective-permute-start | bytes 3932168 | tf_op jit(solution)/shard_map/ppermute | solution.py:637
  18.4 5.0 %collective-permute-start.2 = (f32[72,640]{1,0:T(8,128)S(1)}, f32[72,640]{1,0:T(8,128)S(1)}, u32[]{:S(2)}, u32[]{:S(2)}) collective-permute-start(f32[72,640]{1,0:T(8,128)S(1)} %get-tuple-element.48), channel_id=1, source_target_pairs={{0,8},{1,9},{2,10},{3,11},{4,12},{5,13},{6,14},{7,15},{8,16},{9,17... | collective-permute-start | bytes 552968 | tf_op jit(solution)/shard_map/ppermute | solution.py:609
  18.4 6.0 %collective-permute-start.3 = (f32[72,640]{1,0:T(8,128)S(1)}, f32[72,640]{1,0:T(8,128)S(1)}, u32[]{:S(2)}, u32[]{:S(2)}) collective-permute-start(f32[72,640]{1,0:T(8,128)S(1)} %get-tuple-element.49.after_ref), channel_id=1, source_target_pairs={{0,24},{1,25},{2,26},{3,27},{4,28},{5,29},{6,30},{7,31},{8,0},{9,1... | collective-permute-start | bytes 552968 | tf_op jit(solution)/shard_map/ppermute | solution.py:609
  24.5 8.1 %copy-start.9 = (f32[16,72]{1,0:T(8,128)S(1)}, f32[16,72]{1,0:T(8,128)}, u32[]{:S(2)}) copy-start(f32[16,72]{1,0:T(8,128)} %constant.7.clone.down_map_ref) | copy-start | bytes 13828
  27.8 4.4 %collective-permute-start.4 = (f32[1,72,384]{2,1,0:T(8,128)S(1)}, f32[1,72,384]{2,1,0:T(8,128)S(1)}, u32[]{:S(2)}, u32[]{:S(2)}) collective-permute-start(f32[1,72,384]{2,1,0:T(8,128)S(1)} %get-tuple-element.53), channel_id=1, source_target_pairs={{0,8},{1,9},{2,10},{3,11},{4,12},{5,13},{6,14},{7,15},{8,16},{9,17... | collective-permute-start | bytes 331784 | tf_op jit(solution)/shard_map/ppermute | solution.py:609
  28.5 4.1 %collective-permute-start.5 = (f32[1,72,384]{2,1,0:T(8,128)S(1)}, f32[1,72,384]{2,1,0:T(8,128)S(1)}, u32[]{:S(2)}, u32[]{:S(2)}) collective-permute-start(f32[1,72,384]{2,1,0:T(8,128)S(1)} %get-tuple-element.54), channel_id=1, source_target_pairs={{0,24},{1,25},{2,26},{3,27},{4,28},{5,29},{6,30},{7,31},{8,0},{9,1... | collective-permute-start | bytes 331784 | tf_op jit(solution)/shard_map/ppermute | solution.py:609
  34.4 2.3 %collective-permute-start.8 = (f32[16,128]{1,0:T(8,128)S(1)}, f32[16,128]{1,0:T(8,128)S(1)}, u32[]{:S(2)}, u32[]{:S(2)}) collective-permute-start(f32[16,128]{1,0:T(8,128)S(1)} %get-tuple-element.63.forcing_ref), channel_id=1, source_target_pairs={{0,8},{1,9},{2,10},{3,11},{4,12},{5,13},{6,14},{7,15},{8,0},{9,1},... | collective-permute-start | bytes 24584 | tf_op jit(solution)/shard_map/ppermute | solution.py:637
  67.3 10.3 %collective-permute-start.10 = (bf16[65,40,256]{2,1,0:T(8,128)(2,1)}, bf16[65,40,256]{2,1,0:T(8,128)(2,1)}, u32[]{:S(2)}, u32[]{:S(2)}) collective-permute-start(bf16[65,40,256]{2,1,0:T(8,128)(2,1)} %get-tuple-element.71), channel_id=1, source_target_pairs={{0,8},{1,9},{2,10},{3,11},{4,12},{5,13},{6,14},{7,15},{8,0},{9,1},... | collective-permute-start | bytes 3993608 | tf_op jit(solution)/shard_map/ppermute | solution.py:637
  67.6 2.7 %collective-permute-start.9 = (f32[32,128]{1,0:T(8,128)S(1)}, f32[32,128]{1,0:T(8,128)S(1)}, u32[]{:S(2)}, u32[]{:S(2)}) collective-permute-start(f32[32,128]{1,0:T(8,128)S(1)} %get-tuple-element.65), channel_id=1, source_target_pairs={{0,8},{1,9},{2,10},{3,11},{4,12},{5,13},{6,14},{7,15},{8,0},{9,1},... | collective-permute-start | bytes 49160 | tf_op jit(solution)/shard_map/ppermute | solution.py:637
  71.7 13.6 %all-to-all-start = ((bf16[32,16,128]{2,1,0:T(8,128)(2,1)}), bf16[32,16,128]{2,1,0:T(8,128)(2,1)S(1)}, u32[]{:S(2)}, u32[]{:S(2)}) async-start(bf16[32,16,128]{2,1,0:T(8,128)(2,1)} %get-tuple-element.69), calls=%async_computation | async-start | bytes 262144 | tf_op jit(solution)/shard_map/all_to_all | solution.py:724
  79.5 5.8 %copy-start.8 = (f32[72,16]{1,0:T(8,128)S(1)}, f32[72,16]{1,0:T(8,128)}, u32[]{:S(2)}) copy-start(f32[72,16]{1,0:T(8,128)} %constant.8.clone.up_map_ref) | copy-start | bytes 13828
where the time goes:
time: 86.7 us; the launch traced here: 87.1 us
  Pallas kernels  49 us (57%)
  starting transfers between devices  18.3 us (21%)
  waiting for transfers between devices  14.1 us (16%)
  local copies, waits for them, and re-layouts  4.86 us (6%)
    pallas_call x11, Pallas kernels, call(): pl.pallas_call(kernel, out_shape=[jax.ShapeDtypeStruct(s, t) for s, t in...  49 us
    ppermute x6, starting transfers between devices, shift(): return lax.ppermute(value, ('gcm', 'crm'), pairs)  9.87 us
    ppermute x6, waiting for transfers between devices, shift(): return lax.ppermute(value, ('gcm', 'crm'), pairs)  6.75 us
    all_to_all x1, starting transfers between devices, shards(): lax.all_to_all(send, ('gcm', 'crm'), split_axis=0, concat_axis=0, tiled=T...  5.89 us
    all_to_all x1, waiting for transfers between devices, shards(): lax.all_to_all(send, ('gcm', 'crm'), split_axis=0, concat_axis=0, tiled=T...  3.91 us
    ppermute x5, waiting for transfers between devices, to_partner(): return lax.ppermute(value, ('gcm', 'crm'), pairs)  3.41 us
    unnamed x27, local copies, waits for them, and re-layouts  3.02 us
    ppermute x5, starting transfers between devices, to_partner(): return lax.ppermute(value, ('gcm', 'crm'), pairs)  2.53 us
  transfers between devices with their start and end apart: 12, of which 7 were waited for; matrix products, arithmetic and copies ran while one was open for 5% of the time, Pallas kernels for 12%

commit v1 on v0

--- a/solution.py
+++ b/solution.py
@@ -335,7 +335,7 @@
     slot_ref[...] = owner_ref[...] * capacity + earlier.astype(jnp.int32)
 
 
-def gather_kernel(sent_ref, drops_ref, out_ref, wide_ref):
+def gather_kernel(sent_ref, drops_ref, above_ref, below_ref, out_ref, wide_ref):
     bins = drops_ref.shape[1]
     wide_ref[...] = jnp.zeros(wide_ref.shape, F32)
 
@@ -666,15 +666,18 @@
         [strip] * 4 + [((levels, wide + col_count), F32)] * 2,
         v(from_left, from_right, top, bot),
     )
+    drops, _ = lax.optimization_barrier((drops, top))
     sent, order, force, ordered, rank, slot = call(
         functools.partial(plan_kernel, capacity),
         [row] * 6,
         v(count_row, other_counts, owner.T) + [("h", top)],
     )
+    from_above = shift(bot, 1, 0)
+    from_below = shift(top, -1, 0)
     (leaving,) = call(
         gather_kernel,
         [((guests, 40, cells), BF16)],
-        [("s", sent)] + v(drops),
+        [("s", sent)] + v(drops) + [("h", from_above), ("h", from_below)],
         [((8, 40, cells), F32)],
     )
     guest_drops = to_partner(leaving)
@@ -688,7 +691,7 @@
         second_kernel,
         [field, field, ((levels, row_count, wide), F32)] + [((1, levels, wide), F32)] * 2,
         v(tracer, wind_x, wind_y, tend, q_strip, u_strip, v_strip, tend_strip)
-        + v(shift(bot, 1, 0), shift(top, -1, 0)),
+        + v(from_above, from_below),
     )
     base, forcing = call(
         third_kernel,

time: 86.7 us -> 88.7 us (1.023)
  starting transfers between devices: 18.3 us -> 37.5 us
  Pallas kernels: 49 us -> 30.3 us
  local copies, waits for them, and re-layouts: 4.86 us -> 6.62 us
    all_to_all x1, starting transfers between devices: 5.89 us -> 25 us  [shards(): lax.all_to_all(send, ('gcm', 'crm'), split_axis=0, concat_axis=0, tiled=T...]
    pallas_call x11, Pallas kernels: 49 us -> 30.3 us  [call(): pl.pallas_call(kernel, out_shape=[jax.ShapeDtypeStruct(s, t) for s, t in...]
    optimization_barrier x0 -> x1, local copies, waits for them, and re-layouts: none -> 2.88 us  [shards(): drops, _ = lax.optimization_barrier((drops, top))]
    unnamed x27 -> x26, local copies, waits for them, and re-layouts: 3.02 us -> 1.89 us
  transfers between devices with their start and end apart: 12 -> 12, of which waited for: 7 -> 8; matrix products, arithmetic and copies ran while one was open for 5% -> 5% of each run, Pallas kernels for 12% -> 10%
where the time goes in v1:
time: 88.7 us; the launch traced here: 88.6 us
  starting transfers between devices  37.5 us (42%)
  Pallas kernels  30.3 us (34%)
  waiting for transfers between devices  13.5 us (15%)
  local copies, waits for them, and re-layouts  6.62 us (7%)
    pallas_call x11, Pallas kernels, call(): pl.pallas_call(kernel, out_shape=[jax.ShapeDtypeStruct(s, t) for s, t in...  30.3 us
    all_to_all x1, starting transfers between devices, shards(): lax.all_to_all(send, ('gcm', 'crm'), split_axis=0, concat_axis=0, tiled=T...  25 us
    ppermute x6, starting transfers between devices, shift(): return lax.ppermute(value, ('gcm', 'crm'), pairs)  9.68 us
    ppermute x6, waiting for transfers between devices, shift(): return lax.ppermute(value, ('gcm', 'crm'), pairs)  6.14 us
    all_to_all x1, waiting for transfers between devices, shards(): lax.all_to_all(send, ('gcm', 'crm'), split_axis=0, concat_axis=0, tiled=T...  3.91 us
    ppermute x5, waiting for transfers between devices, to_partner(): return lax.ppermute(value, ('gcm', 'crm'), pairs)  3.41 us
    optimization_barrier x1, local copies, waits for them, and re-layouts, shards(): drops, _ = lax.optimization_barrier((drops, top))  2.88 us
    ppermute x5, starting transfers between devices, to_partner(): return lax.ppermute(value, ('gcm', 'crm'), pairs)  2.83 us
  transfers between devices with their start and end apart: 12, of which 8 were waited for; matrix products, arithmetic and copies ran while one was open for 5% of the time, Pallas kernels for 10%

profile of v1, /device:TPU:0, one launch (start us, length us, event | category | flops | bytes accessed | tf_op | source)
XLA Modules:
  0.0 88.6 jit_solution(12593890692604030001)
XLA Ops:
  0.6 4.8 %shard_map.130 = (f32[72,8,256]{2,1,0:T(8,128)}, f32[2,72,256]{2,1,0:T(8,128)}, f32[2,72,256]{2,1,0:T(8,128)}, f32[18,8,128]{2,1,0:T(8,128)}, f32[18,8,128]{2,1,0:T(8,128)}, /*index=5*/s32[1,128]{1,0:T(1,128)}) custom-call(f32[72,8,256]{2,1,0:T(8,128)} %q_ref.3, f32[72,8,256]{2,1,0:T(8,128)} %u_ref.1, f32[72,8,256]{2,1,0:T(8,128)} %v_ref.1, s32[1,128]{1,0:T(1,128)} %bitcast.11), custom_call_target="tpu_custom_call" | custom-call | flops 10000000 | bytes 4000000 | tf_op jit(solution)/shard_map/pallas_call | solution.py:584
  5.4 3.0 %collective-permute-start = (f32[18,8,128]{2,1,0:T(8,128)}, f32[18,8,128]{2,1,0:T(8,128)S(1)}, u32[]{:S(2)}, u32[]{:S(2)}) collective-permute-start(f32[18,8,128]{2,1,0:T(8,128)} %get-tuple-element.41), channel_id=1, source_target_pairs={{0,1},{1,2},{2,3},{3,4},{4,5},{5,6},{6,7},{7,0},{8,9},{9,10},{10,1... | collective-permute-start | bytes 221192 | tf_op jit(solution)/shard_map/ppermute | solution.py:609
  8.4 3.1 %collective-permute-start.1 = (f32[18,8,128]{2,1,0:T(8,128)}, f32[18,8,128]{2,1,0:T(8,128)S(1)}, u32[]{:S(2)}, u32[]{:S(2)}) collective-permute-start(f32[18,8,128]{2,1,0:T(8,128)} %get-tuple-element.42), channel_id=1, source_target_pairs={{0,7},{1,0},{2,1},{3,2},{4,3},{5,4},{6,5},{7,6},{8,15},{9,8},{10,9... | collective-permute-start | bytes 221192 | tf_op jit(solution)/shard_map/ppermute | solution.py:609
  11.5 2.5 %collective-permute-done.left_ref = f32[18,8,128]{2,1,0:T(8,128)S(1)} collective-permute-done((f32[18,8,128]{2,1,0:T(8,128)}, f32[18,8,128]{2,1,0:T(8,128)S(1)}, u32[]{:S(2)}, u32[]{:S(2)}) %collective-permute-start) | collective-permute-done | bytes 73760 | tf_op jit(solution)/shard_map/ppermute | solution.py:609
  14.1 0.5 collective-permute-done.1.right_ref
  14.6 0.9 %copy-done.5 = f32[2,72,256]{2,1,0:T(8,128)S(1)} copy-done((f32[2,72,256]{2,1,0:T(8,128)S(1)}, f32[2,72,256]{2,1,0:T(8,128)}, u32[]{:S(2)}) %copy-start.5) | copy-done | bytes 147480
  15.5 0.9 %copy-done.6 = f32[2,72,256]{2,1,0:T(8,128)S(1)} copy-done((f32[2,72,256]{2,1,0:T(8,128)S(1)}, f32[2,72,256]{2,1,0:T(8,128)}, u32[]{:S(2)}) %copy-start.6) | copy-done | bytes 147480
  16.4 2.0 %shard_map.131 = (f32[72,8,128]{2,1,0:T(8,128)S(1)}, f32[72,8,128]{2,1,0:T(8,128)S(1)}, f32[72,8,128]{2,1,0:T(8,128)S(1)}, f32[72,8,128]{2,1,0:T(8,128)S(1)}, f3...) custom-call(f32[18,8,128]{2,1,0:T(8,128)S(1)} %collective-permute-done.left_ref, ...), custom_call_target="tpu_custom_call" | custom-call | flops 10000000 | bytes 4000000 | tf_op jit(solution)/shard_map/pallas_call | solution.py:584
  18.4 0.1 collective-permute-start.2
  18.5 1.7 %collective-permute-start.3 = (f32[72,640]{1,0:T(8,128)S(1)}, f32[72,640]{1,0:T(8,128)S(1)}, u32[]{:S(2)}, u32[]{:S(2)}) collective-permute-start(f32[72,640]{1,0:T(8,128)S(1)} %get-tuple-element.50.after_ref), channel_id=1, source_target_pairs={{0,24},{1,25},{2,26},{3,27},{4,28},{5,29},{6,30},{7,31},{8,0},{9,1... | collective-permute-start | bytes 552968 | tf_op jit(solution)/shard_map/ppermute | solution.py:609
  20.2 0.0 collective-permute-start.6
  20.2 2.9 %copy.16.drops_ref = bf16[128,33,256]{2,1,0:T(8,128)(2,1)S(1)} copy(bf16[128,33,256]{2,0,1:T(8,128)(2,1)} %param.14) | data formatting | bytes 4325376 | tf_op jit(solution)/shard_map/optimization_barrier | solution.py:669
  23.1 0.0 collective-permute-done.6.other_ref
  23.1 0.4 shard_map.135
  23.5 0.0 copy-start
  23.5 0.0 copy-start.1
  23.6 0.0 copy-start.2
  23.6 0.0 copy-start.4
  23.6 0.0 collective-permute-done.2.up_ref.above_ref
  23.6 0.8 collective-permute-done.3.down_ref.below_ref
  24.4 0.7 shard_map.136
  25.2 0.0 copy-start.3
  25.2 0.0 copy-start.7
  25.2 0.0 copy-start.11
  25.2 0.8 collective-permute-start.7
  26.1 0.0 copy-start.9
  26.1 3.3 %shard_map.132 = (f32[72,8,256]{2,1,0:T(8,128)S(1)}, f32[72,8,256]{2,1,0:T(8,128)S(1)}, f32[72,8,384]{2,1,0:T(8,128)S(1)}, f32[1,72,384]{2,1,0:T(8,128)S(1)}, f32[1,72,384]{2,1,0:T(8,128)S(1)}) custom-call(f32[72,8,256]{2,1,0:T(8,128)S(1)} %copy-done, f32[72,8,256]{2,1,0:T(8,128)S(1)} %copy-done.1, f32[72,8,256]{2,1,0:T(8,128)S(1)} %copy-done.2, ...), custom_call_target="tpu_custom_call" | custom-call | flops 10000000 | bytes 4000000 | tf_op jit(solution)/shard_map/pallas_call | solution.py:584
  29.4 0.1 collective-permute-start.4
  29.5 1.7 %collective-permute-start.5 = (f32[1,72,384]{2,1,0:T(8,128)S(1)}, f32[1,72,384]{2,1,0:T(8,128)S(1)}, u32[]{:S(2)}, u32[]{:S(2)}) collective-permute-start(f32[1,72,384]{2,1,0:T(8,128)S(1)} %get-tuple-element.55), channel_id=1, source_target_pairs={{0,24},{1,25},{2,26},{3,27},{4,28},{5,29},{6,30},{7,31},{8,0},{9,1... | collective-permute-start | bytes 331784 | tf_op jit(solution)/shard_map/ppermute | solution.py:609
  31.2 0.4 shard_map.133
  31.6 2.0 %collective-permute-done.4.up_ref = f32[1,72,384]{2,1,0:T(8,128)S(1)} collective-permute-done((f32[1,72,384]{2,1,0:T(8,128)S(1)}, f32[1,72,384]{2,1,0:T(8,128)S(1)}, u32[]{:S(2)}, u32[]{:S(2)}) %collective-permute-start.4) | collective-permute-done | bytes 110624 | tf_op jit(solution)/shard_map/ppermute | solution.py:609
  33.6 0.2 collective-permute-done.5.down_ref
  33.8 1.8 %shard_map.134 = (f32[72,8,256]{2,1,0:T(8,128)S(1)}, f32[16,128]{1,0:T(8,128)S(1)}) custom-call(f32[72,8,256]{2,1,0:T(8,128)S(1)} %copy-done, f32[72,8,256]{2,1,0:T(8,128)S(1)} %get-tuple-element.51.state_ref, f32[72,8,256]{2,1,0:T(8,128)S(1)} %get-tuple-element.52.smooth_ref, f32[72,8,384]{2,1,0:T(8,128)S(1)} %get-tuple-element.53.tend_ref, ...), custom_call_target="tpu_custom_call" | custom-call | flops 10000000 | bytes 4000000 | tf_op jit(solution)/shard_map/pallas_call | solution.py:584
  35.6 1.5 %collective-permute-start.8 = (f32[16,128]{1,0:T(8,128)S(1)}, f32[16,128]{1,0:T(8,128)S(1)}, u32[]{:S(2)}, u32[]{:S(2)}) collective-permute-start(f32[16,128]{1,0:T(8,128)S(1)} %get-tuple-element.65.forcing_ref), channel_id=1, source_target_pairs={{0,8},{1,9},{2,10},{3,11},{4,12},{5,13},{6,14},{7,15},{8,0},{9,1},... | collective-permute-start | bytes 24584 | tf_op jit(solution)/shard_map/ppermute | solution.py:637
  37.0 0.8 collective-permute-done.8.other_ref
  37.9 0.0 collective-permute-done.7.guest_ref
  37.9 11.9 %shard_map.137 = (bf16[128,33,256]{2,1,0:T(8,128)(2,1)S(1)}, bf16[65,40,256]{2,1,0:T(8,128)(2,1)}, f32[32,128]{1,0:T(8,128)S(1)}, f32[32,128]{1,0:T(8,128)S(1)}) custom-call(s32[1,128]{1,0:T(1,128)S(1)} %get-tuple-element.60.order_ref, s32[1,128]{1,0:T(1,128)S(1)} %get-tuple-element.61.force_ref, s32[1,128]{1,0:T(1,128)S(1)} %get-tuple-element.62.count_ref, ...), custom_call_target="tpu_custom_call" | custom-call | flops 10000000000 | bytes 4000000 | tf_op jit(solution)/shard_map/pallas_call | solution.py:584
  49.8 0.3 collective-permute-start.10
  50.1 0.2 collective-permute-start.9
  50.3 2.6 %collective-permute-done.9.back_ref = f32[32,128]{1,0:T(8,128)S(1)} collective-permute-done((f32[32,128]{1,0:T(8,128)S(1)}, f32[32,128]{1,0:T(8,128)S(1)}, u32[]{:S(2)}, u32[]{:S(2)}) %collective-permute-start.9) | collective-permute-done | bytes 16416 | tf_op jit(solution)/shard_map/ppermute | solution.py:637
  52.9 1.3 %shard_map.138 = (f32[16,128]{1,0:T(8,128)S(1)}, bf16[32,16,128]{2,1,0:T(8,128)(2,1)}) custom-call(f32[32,128]{1,0:T(8,128)S(1)} %get-tuple-element.66.own_ref, f32[32,128]{1,0:T(8,128)S(1)} %collective-permute-done.9.back_ref, s32[1,128]{1,0:T(1,128)S(1)} %get-tuple-element.68.rank_ref, s32[1,128]{1,0:T(1,128)S(1)} %get-tuple-element.69.slot_ref), custom_call_target="tpu_custom_call" | custom-call | flops 10000000 | bytes 4000000 | tf_op jit(solution)/shard_map/pallas_call | solution.py:584
  54.2 25.0 %all-to-all-start = ((bf16[32,16,128]{2,1,0:T(8,128)(2,1)}), bf16[32,16,128]{2,1,0:T(8,128)(2,1)S(1)}, u32[]{:S(2)}, u32[]{:S(2)}) async-start(bf16[32,16,128]{2,1,0:T(8,128)(2,1)} %get-tuple-element.71), calls=%async_computation | async-start | bytes 262144 | tf_op jit(solution)/shard_map/all_to_all | solution.py:727
  79.1 0.0 collective-permute-done.10.back_ref
  79.1 2.0 %shard_map.139 = bf16[128,33,256]{2,1,0:T(8,128)(2,1)S(1)} custom-call(s32[1,128]{1,0:T(1,128)S(1)} %get-tuple-element.63.sent_ref, bf16[128,33,256]{2,1,0:T(8,128)(2,1)S(1)} %get-tuple-element.72.final_ref, bf16[65,40,256]{2,1,0:T(8,128)(2,1)} %collective-permute-done.10.back_ref), custom_call_target="tpu_custom_call" | custom-call | flops 10000000 | bytes 4000000 | tf_op jit(solution)/shard_map/pallas_call | solution.py:584
  81.1 0.0 copy-start.8
  81.1 1.8 %copy.19 = bf16[128,33,256]{2,0,1:T(8,128)(2,1)} copy(bf16[128,33,256]{2,1,0:T(8,128)(2,1)S(1)} %shard_map.139) | data formatting | bytes 4325376 | tf_op jit(solution)/shard_map/pallas_call | solution.py:584
  83.0 3.9 %all-to-all-done.got_ref = bf16[32,16,128]{2,1,0:T(8,128)(2,1)S(1)} async-done(((bf16[32,16,128]{2,1,0:T(8,128)(2,1)}), bf16[32,16,128]{2,1,0:T(8,128)(2,1)S(1)}, u32[]{:S(2)}, u32[]{:S(2)}) %all-to-all-start) | async-done | bytes 131104 | tf_op jit(solution)/shard_map/all_to_all | solution.py:727
  86.9 1.8 %shard_map.140 = (f32[72,8,256]{2,1,0:T(8,128)}, f32[16,256]{1,0:T(8,128)}, bf16[33,128,256]{2,1,0:T(8,128)(2,1)}) custom-call(f32[72,8,256]{2,1,0:T(8,128)S(1)} %get-tuple-element.58.base_ref, f32[16,128]{1,0:T(8,128)S(1)} %get-tuple-element.70.own_ref, bf16[32,16,128]{2,1,0:T(8,128)(2,1)S(1)} %all-to-all-done.got_ref, ...), custom_call_target="tpu_custom_call", output_to_operand_aliasing={{2}: (4, {})} | custom-call | flops 10000000 | bytes 4000000 | tf_op jit(solution)/shard_map/pallas_call | solution.py:584
  (15 shorter events, 0.0 us)
Async XLA Ops:
  5.4 8.6 %collective-permute-start = (f32[18,8,128]{2,1,0:T(8,128)}, f32[18,8,128]{2,1,0:T(8,128)S(1)}, u32[]{:S(2)}, u32[]{:S(2)}) collective-permute-start(f32[18,8,128]{2,1,0:T(8,128)} %get-tuple-element.41), channel_id=1, source_target_pairs={{0,1},{1,2},{2,3},{3,4},{4,5},{5,6},{6,7},{7,0},{8,9},{9,10},{10,1... | collective-permute-start | bytes 221192 | tf_op jit(solution)/shard_map/ppermute | solution.py:609
  8.4 6.1 %collective-permute-start.1 = (f32[18,8,128]{2,1,0:T(8,128)}, f32[18,8,128]{2,1,0:T(8,128)S(1)}, u32[]{:S(2)}, u32[]{:S(2)}) collective-permute-start(f32[18,8,128]{2,1,0:T(8,128)} %get-tuple-element.42), channel_id=1, source_target_pairs={{0,7},{1,0},{2,1},{3,2},{4,3},{5,4},{6,5},{7,6},{8,15},{9,8},{10,9... | collective-permute-start | bytes 221192 | tf_op jit(solution)/shard_map/ppermute | solution.py:609
  14.6 0.9 %copy-start.5 = (f32[2,72,256]{2,1,0:T(8,128)S(1)}, f32[2,72,256]{2,1,0:T(8,128)}, u32[]{:S(2)}) copy-start(f32[2,72,256]{2,1,0:T(8,128)} %get-tuple-element.43.top_main) | copy-start | bytes 442372
  15.5 0.9 %copy-start.6 = (f32[2,72,256]{2,1,0:T(8,128)S(1)}, f32[2,72,256]{2,1,0:T(8,128)}, u32[]{:S(2)}) copy-start(f32[2,72,256]{2,1,0:T(8,128)} %get-tuple-element.44.bot_main) | copy-start | bytes 442372
  18.4 5.2 %collective-permute-start.2 = (f32[72,640]{1,0:T(8,128)S(1)}, f32[72,640]{1,0:T(8,128)S(1)}, u32[]{:S(2)}, u32[]{:S(2)}) collective-permute-start(f32[72,640]{1,0:T(8,128)S(1)} %get-tuple-element.49), channel_id=1, source_target_pairs={{0,8},{1,9},{2,10},{3,11},{4,12},{5,13},{6,14},{7,15},{8,16},{9,17... | collective-permute-start | bytes 552968 | tf_op jit(solution)/shard_map/ppermute | solution.py:609
  18.5 6.0 %collective-permute-start.3 = (f32[72,640]{1,0:T(8,128)S(1)}, f32[72,640]{1,0:T(8,128)S(1)}, u32[]{:S(2)}, u32[]{:S(2)}) collective-permute-start(f32[72,640]{1,0:T(8,128)S(1)} %get-tuple-element.50.after_ref), channel_id=1, source_target_pairs={{0,24},{1,25},{2,26},{3,27},{4,28},{5,29},{6,30},{7,31},{8,0},{9,1... | collective-permute-start | bytes 552968 | tf_op jit(solution)/shard_map/ppermute | solution.py:609
  20.2 2.9 %copy-start.10 = (s32[128,1]{0,1:T(1,128)S(1)}, s32[128,1]{0,1:T(1,128)}, u32[]{:S(2)}) copy-start(s32[128,1]{0,1:T(1,128)} %param.15) | copy-start | bytes 1540
  20.2 2.9 %copy-start.12 = (s32[1,128]{1,0:T(1,128)S(1)}, s32[1,128]{1,0:T(1,128)}, u32[]{:S(2)}) copy-start(s32[1,128]{1,0:T(1,128)} %get-tuple-element.59.count_ref) | copy-start | bytes 1540
  20.2 2.9 %collective-permute-start.6 = (s32[1,128]{1,0:T(1,128)}, s32[1,128]{1,0:T(1,128)S(1)}, u32[]{:S(2)}, u32[]{:S(2)}) collective-permute-start(s32[1,128]{1,0:T(1,128)} %get-tuple-element.59.count_ref), channel_id=1, source_target_pairs={{0,8},{1,9},{2,10},{3,11},{4,12},{5,13},{6,14},{7,15},{8,0},{9,1},... | collective-permute-start | bytes 1544 | tf_op jit(solution)/shard_map/ppermute | solution.py:637
  23.5 2.5 %copy-start = (f32[72,8,256]{2,1,0:T(8,128)S(1)}, f32[72,8,256]{2,1,0:T(8,128)}, u32[]{:S(2)}) copy-start(f32[72,8,256]{2,1,0:T(8,128)} %q_ref.3) | copy-start | bytes 1769476
  23.5 2.5 %copy-start.1 = (f32[72,8,256]{2,1,0:T(8,128)S(1)}, f32[72,8,256]{2,1,0:T(8,128)}, u32[]{:S(2)}) copy-start(f32[72,8,256]{2,1,0:T(8,128)} %u_ref.1) | copy-start | bytes 1769476
  23.6 2.5 %copy-start.2 = (f32[72,8,256]{2,1,0:T(8,128)S(1)}, f32[72,8,256]{2,1,0:T(8,128)}, u32[]{:S(2)}) copy-start(f32[72,8,256]{2,1,0:T(8,128)} %v_ref.1) | copy-start | bytes 1769476
  23.6 2.5 %copy-start.4 = (f32[72,8,256]{2,1,0:T(8,128)S(1)}, f32[72,8,256]{2,1,0:T(8,128)}, u32[]{:S(2)}) copy-start(f32[72,8,256]{2,1,0:T(8,128)} %get-tuple-element.40.tend_ref) | copy-start | bytes 1769476
  25.2 6.0 %copy-start.3 = (bf16[1089,576]{1,0:T(8,128)(2,1)S(1)}, bf16[1089,576]{1,0:T(8,128)(2,1)}, u32[]{:S(2)}) copy-start(bf16[1089,576]{1,0:T(8,128)(2,1)} %constant.6.clone.table_ref) | copy-start | bytes 3763588
  25.2 6.0 %copy-start.7 = (bf16[33,1089]{1,0:T(8,128)(2,1)S(1)}, bf16[33,1089]{1,0:T(8,128)(2,1)}, u32[]{:S(2)}) copy-start(bf16[33,1089]{1,0:T(8,128)(2,1)} %collision_ref.1) | copy-start | bytes 215626
  25.2 6.0 %copy-start.11 = (f32[33]{0:T(128)S(1)}, f32[33]{0:T(128)}, u32[]{:S(2)}) copy-start(f32[33]{0:T(128)} %param.18) | copy-start | bytes 400
  25.2 12.7 %collective-permute-start.7 = (bf16[64,40,256]{2,1,0:T(8,128)(2,1)S(1)}, bf16[64,40,256]{2,1,0:T(8,128)(2,1)S(1)}, u32[]{:S(2)}, u32[]{:S(2)}) collective-permute-start(bf16[64,40,256]{2,1,0:T(8,128)(2,1)S(1)} %shard_map.136), channel_id=1, source_target_pairs={{0,8},{1,9},{2,10},{3,11},{4,12},{5,13},{6,14},{7,15},{8,0},{9,1},... | collective-permute-start | bytes 3932168 | tf_op jit(solution)/shard_map/ppermute | solution.py:637
  26.1 7.8 %copy-start.9 = (f32[16,72]{1,0:T(8,128)S(1)}, f32[16,72]{1,0:T(8,128)}, u32[]{:S(2)}) copy-start(f32[16,72]{1,0:T(8,128)} %constant.7.clone.down_map_ref) | copy-start | bytes 13828
  29.4 4.2 %collective-permute-start.4 = (f32[1,72,384]{2,1,0:T(8,128)S(1)}, f32[1,72,384]{2,1,0:T(8,128)S(1)}, u32[]{:S(2)}, u32[]{:S(2)}) collective-permute-start(f32[1,72,384]{2,1,0:T(8,128)S(1)} %get-tuple-element.54), channel_id=1, source_target_pairs={{0,8},{1,9},{2,10},{3,11},{4,12},{5,13},{6,14},{7,15},{8,16},{9,17... | collective-permute-start | bytes 331784 | tf_op jit(solution)/shard_map/ppermute | solution.py:609
  29.5 4.4 %collective-permute-start.5 = (f32[1,72,384]{2,1,0:T(8,128)S(1)}, f32[1,72,384]{2,1,0:T(8,128)S(1)}, u32[]{:S(2)}, u32[]{:S(2)}) collective-permute-start(f32[1,72,384]{2,1,0:T(8,128)S(1)} %get-tuple-element.55), channel_id=1, source_target_pairs={{0,24},{1,25},{2,26},{3,27},{4,28},{5,29},{6,30},{7,31},{8,0},{9,1... | collective-permute-start | bytes 331784 | tf_op jit(solution)/shard_map/ppermute | solution.py:609
  35.6 2.3 %collective-permute-start.8 = (f32[16,128]{1,0:T(8,128)S(1)}, f32[16,128]{1,0:T(8,128)S(1)}, u32[]{:S(2)}, u32[]{:S(2)}) collective-permute-start(f32[16,128]{1,0:T(8,128)S(1)} %get-tuple-element.65.forcing_ref), channel_id=1, source_target_pairs={{0,8},{1,9},{2,10},{3,11},{4,12},{5,13},{6,14},{7,15},{8,0},{9,1},... | collective-permute-start | bytes 24584 | tf_op jit(solution)/shard_map/ppermute | solution.py:637
  49.8 29.4 %collective-permute-start.10 = (bf16[65,40,256]{2,1,0:T(8,128)(2,1)}, bf16[65,40,256]{2,1,0:T(8,128)(2,1)}, u32[]{:S(2)}, u32[]{:S(2)}) collective-permute-start(bf16[65,40,256]{2,1,0:T(8,128)(2,1)} %get-tuple-element.73), channel_id=1, source_target_pairs={{0,8},{1,9},{2,10},{3,11},{4,12},{5,13},{6,14},{7,15},{8,0},{9,1},... | collective-permute-start | bytes 3993608 | tf_op jit(solution)/shard_map/ppermute | solution.py:637
  50.1 2.7 %collective-permute-start.9 = (f32[32,128]{1,0:T(8,128)S(1)}, f32[32,128]{1,0:T(8,128)S(1)}, u32[]{:S(2)}, u32[]{:S(2)}) collective-permute-start(f32[32,128]{1,0:T(8,128)S(1)} %get-tuple-element.67), channel_id=1, source_target_pairs={{0,8},{1,9},{2,10},{3,11},{4,12},{5,13},{6,14},{7,15},{8,0},{9,1},... | collective-permute-start | bytes 49160 | tf_op jit(solution)/shard_map/ppermute | solution.py:637
  54.2 32.7 %all-to-all-start = ((bf16[32,16,128]{2,1,0:T(8,128)(2,1)}), bf16[32,16,128]{2,1,0:T(8,128)(2,1)S(1)}, u32[]{:S(2)}, u32[]{:S(2)}) async-start(bf16[32,16,128]{2,1,0:T(8,128)(2,1)} %get-tuple-element.71), calls=%async_computation | async-start | bytes 262144 | tf_op jit(solution)/shard_map/all_to_all | solution.py:727
  81.1 5.8 %copy-start.8 = (f32[72,16]{1,0:T(8,128)S(1)}, f32[72,16]{1,0:T(8,128)}, u32[]{:S(2)}) copy-start(f32[72,16]{1,0:T(8,128)} %constant.8.clone.up_map_ref) | copy-start | bytes 13828
